TPU v7x, 32 devices: a whole 2x2x4 slice. The times are simulated.
32 devices in a mesh: frames: 8 (over y, x, core), rows: 4 (over z).
Axes of the slice: x: 2, y: 2, z: 4, core: 2. Of those that a mesh axis runs over, the one named last changes fastest.
Arguments:
- input_feature_maps: float32 [96, 16, 16, 1024], P('frames', 'rows'), may hold values from -6 to 6
- sequence_slot_lookup: int32 [96], P('frames'), may hold values from 0 to 31, as said below
- sequence_span_lookup: int32 [96], P('frames'), may hold values from 8 to 32, as said below
- opening_reducer: bfloat16 [1024, 512], replicated, may hold values from -0.1875 to 0.1875
- downsampling_filter: bfloat16 [3, 3, 512, 512], replicated, may hold values from -0.09375 to 0.09375
- opening_expander: bfloat16 [512, 2048], replicated, may hold values from -0.25 to 0.25
- skip_projection: bfloat16 [1024, 2048], replicated, may hold values from -0.1875 to 0.1875
- closing_reducer: bfloat16 [2048, 512], replicated, may hold values from -0.125 to 0.125
- excite_reducer: bfloat16 [512, 32], replicated, may hold values from -0.25 to 0.25
- excite_spatial_filter: bfloat16 [3, 3, 32, 32], replicated, may hold values from -0.375 to 0.375
- excite_expander: bfloat16 [32, 512], replicated, may hold values from -4 to 4
- time_taps: bfloat16 [3, 384], replicated, may hold values from 0.19921875 to 0.796875
- spatial_filters: bfloat16 [3, 3, 3, 128, 128], replicated, may hold values from -0.1875 to 0.1875
- closing_expander: bfloat16 [512, 2048], replicated, may hold values from -0.25 to 0.25
- narrow_norm_gains: float32 [4, 512], replicated, may hold values from 0.5 to 1.5
- narrow_norm_biases: float32 [4, 512], replicated, may hold values from -3 to 3
- wide_norm_gains: float32 [3, 2048], replicated, may hold values from 0.5 to 1.5
- wide_norm_biases: float32 [3, 2048], replicated, may hold values from -3 to 3
- loss_slope_wrt_final: float32 [96, 8, 8, 2048], P('frames', 'rows'), may hold values from -6 to 6
Outputs:
- layer_output: float32 [96, 8, 8, 2048], P('frames', 'rows')
- grad_pixels: float32 [96, 16, 16, 1024], P('frames', 'rows')
- grad_narrower: float32 [1024, 512], P(None, 'rows')
- grad_strider: float32 [3, 3, 512, 512], P(None, None, None, 'rows')
- grad_widener: float32 [512, 2048], P(None, 'rows')
- grad_shortcut: float32 [1024, 2048], P(None, 'rows')
- grad_squeezer: float32 [2048, 512], P(None, 'rows')
- grad_condenser: float32 [512, 32], P(None, 'rows')
- grad_stencil: float32 [3, 3, 32, 32], P(None, None, None, 'rows')
- grad_exciter: float32 [32, 512], P(None, 'rows')
- grad_temporal: float32 [3, 384], P(None, 'rows')
- grad_kernels: float32 [3, 3, 3, 128, 128], P(None, None, None, None, 'rows')
- grad_restorer: float32 [512, 2048], P(None, 'rows')
- grad_scaling: float32 [4, 512], replicated
- grad_biasing: float32 [4, 512], replicated
- grad_amplitudes: float32 [3, 2048], replicated
- baseline_gradient: float32 [3, 2048], replicated
Inputs may be any that keep to these rules, and one draw needn't show every extreme that they name: `sequence_slot_lookup`: the offset of each frame within its clip. Clips are runs of 8 or 32 frames laid end to end from frame 0; each aligned run of 96 frames holds one clip of 32 frames and eight of 8. `sequence_span_lookup`: the length of the clip that holds each frame, consistent with sequence_slot_lookup.
All inputs are finite; a program needn't handle non-finite values.
Results may differ from a plain program's by a relative error of at most 0.0003.
Values sent between devices are 32-bit elements; how exact they have to be, the bound alone decides.
A program may use at most 192 MiB of HBM per device.

v0:
```python
import jax
import jax.numpy as jnp
from jax import lax
from jax.experimental import pallas as pl
from jax.experimental.pallas import tpu as pltpu
from jax.sharding import PartitionSpec as P

HIGHEST = lax.Precision.HIGH
MESH = pl.DeviceIdType.MESH
EPSILON = 1e-05
LAYOUT = ("NHWC", "HWIO", "NHWC")


def with_halo(block, sides, width):
    for axis, dim in sides:
        count = lax.axis_size(axis)
        forward = [(i, i + 1) for i in range(count - 1)]
        backward = [(target, source) for source, target in forward]
        low = lax.ppermute(
            lax.slice_in_dim(block, block.shape[dim] - width, None, axis=dim), axis, forward
        )
        high = lax.ppermute(lax.slice_in_dim(block, 0, width, axis=dim), axis, backward)
        block = jnp.concatenate([low, block, high], axis=dim)
    return block


def from_behind(block, axis, distance):
    devices = range(lax.axis_size(axis))
    route = [(i - distance, i) for i in devices if i - distance in devices]
    return lax.ppermute(block, axis, route)


def logistic_squash(value):
    return value * jax.nn.sigmoid(value)


def unit_slope(value):
    logistic = jax.nn.sigmoid(value)
    return logistic * (1.0 + value * (1.0 - logistic))


def pointwise_mapping(active, matrix):
    return jnp.einsum("fhwc,cd->fhwd", active, matrix, precision=HIGHEST)


def project_back(grads, matrix):
    return jnp.einsum("fhwd,cd->fhwc", grads, matrix, precision=HIGHEST)


def outer_sum(active, grads):
    return jnp.einsum("fhwc,fhwd->cd", active, grads, precision=HIGHEST)


def conv_valid(padded, kernel):
    return lax.conv_general_dilated(
        padded, kernel, (1, 1), ((0, 0), (1, 1)), dimension_numbers=LAYOUT, precision=HIGHEST
    )


def conv_stride(padded, kernel):
    return lax.conv_general_dilated(
        padded, kernel, (2, 2), ((0, 0), (1, 1)), dimension_numbers=LAYOUT, precision=HIGHEST
    )


def kernel_grad(padded, kernel, grads):
    result, pull_back = jax.vjp(lambda weights: conv_valid(padded, weights), kernel)
    return pull_back(grads)[0]


def flipped(kernel):
    return jnp.transpose(kernel[::-1, ::-1], (0, 1, 3, 2))


def row_padded(field):
    return with_halo(field, (("rows", 1),), 1)


def frame_padded(field):
    return with_halo(field, (("frames", 0),), 1)


def time_mix(padded, weights, earlier_boundary_filter, later_boundary_filter):
    return (
        weights[0] * earlier_boundary_filter * padded[:-2]
        + weights[1] * padded[1:-1]
        + weights[2] * later_boundary_filter * padded[2:]
    )


def exchange_slots(source, slots, send, recv, me, count, device):
    copies = []
    for step in range(1, count):
        copy = pltpu.make_async_remote_copy(
            src_ref=source,
            dst_ref=slots.at[me],
            send_sem=send.at[step],
            recv_sem=recv.at[me],
            device_id=device(lax.rem(me + step, count)),
            device_id_type=MESH,
        )
        copy.start()
        copies.append(copy)
    slots[me] = source[...]
    for step in range(1, count):
        origin = lax.rem(me + count - step, count)
        pltpu.make_async_remote_copy(
            src_ref=source,
            dst_ref=slots.at[origin],
            send_sem=send.at[step],
            recv_sem=recv.at[origin],
            device_id=device(origin),
            device_id_type=MESH,
        ).wait_recv()
    for copy in copies:
        copy.wait_send()
    total = slots[0]
    for place in range(1, count):
        total = total + slots[place]
    return total


def sum_kernel(frames, rows, x_ref, o_ref, part, row_slots, frame_slots, rs, rr, fs, fr):
    f = lax.axis_index("frames")
    r = lax.axis_index("rows")
    barrier = pltpu.get_barrier_semaphore()
    for step in range(1, rows):
        pl.semaphore_signal(
            barrier, inc=1, device_id=(f, lax.rem(r + step, rows)), device_id_type=MESH
        )
    for step in range(1, frames):
        pl.semaphore_signal(
            barrier, inc=1, device_id=(lax.rem(f + step, frames), r), device_id_type=MESH
        )
    pl.semaphore_wait(barrier, rows + frames - 2)
    part[...] = exchange_slots(x_ref, row_slots, rs, rr, r, rows, lambda place: (f, place))
    o_ref[...] = exchange_slots(part, frame_slots, fs, fr, f, frames, lambda place: (place, r))


def global_sum(pieces, call):
    frames, rows = lax.axis_size("frames"), lax.axis_size("rows")
    sizes = [piece.size // 128 for piece in pieces]
    block = jnp.concatenate([piece.reshape(-1, 128) for piece in pieces], 0)
    total = pl.pallas_call(
        lambda *refs: sum_kernel(frames, rows, *refs),
        out_shape=jax.ShapeDtypeStruct(block.shape, jnp.float32),
        in_specs=[pl.BlockSpec(memory_space=pltpu.VMEM)],
        out_specs=pl.BlockSpec(memory_space=pltpu.VMEM),
        scratch_shapes=[
            pltpu.VMEM(block.shape, jnp.float32),
            pltpu.VMEM((rows,) + block.shape, jnp.float32),
            pltpu.VMEM((frames,) + block.shape, jnp.float32),
            pltpu.SemaphoreType.DMA((rows,)),
            pltpu.SemaphoreType.DMA((rows,)),
            pltpu.SemaphoreType.DMA((frames,)),
            pltpu.SemaphoreType.DMA((frames,)),
        ],
        compiler_params=pltpu.CompilerParams(collective_id=call, has_side_effects=True),
    )(block)
    results = []
    start = 0
    for piece, size in zip(pieces, sizes):
        results.append(total[start : start + size].reshape(piece.shape))
        start += size
    return results


def global_count(field):
    return (
        field.shape[0]
        * field.shape[1]
        * field.shape[2]
        * lax.axis_size("frames")
        * lax.axis_size("rows")
    )


def norm_forward(field, call):
    totals, squares = global_sum(
        (jnp.sum(field, axis=(0, 1, 2)), jnp.sum(field * field, axis=(0, 1, 2))), call
    )
    number = global_count(field)
    center = totals / number
    spread = lax.rsqrt(squares / number - center * center + EPSILON)
    return ((field - center) * spread, spread)


def norm_backward(grads, normed, spread, gain, call):
    bias_grad, gain_grad = global_sum(
        (jnp.sum(grads, axis=(0, 1, 2)), jnp.sum(grads * normed, axis=(0, 1, 2))), call
    )
    number = global_count(grads)
    field_grad = gain * spread * (grads - bias_grad / number - normed * (gain_grad / number))
    return (field_grad, gain_grad, bias_grad)


def layer_one(
    input_feature_maps,
    opening_reducer,
    downsampling_filter,
    opening_expander,
    skip_projection,
    narrow_norm_gains,
    narrow_norm_biases,
    wide_norm_gains,
    wide_norm_biases,
):
    normed_a, spread_a = norm_forward(pointwise_mapping(input_feature_maps, opening_reducer), 0)
    before_a = normed_a * narrow_norm_gains[0] + narrow_norm_biases[0]
    hidden_a = logistic_squash(before_a)
    upper_rim = from_behind(hidden_a[:, -1:], "rows", 1)
    padded_a = jnp.concatenate([upper_rim, hidden_a], 1)
    normed_b, spread_b = norm_forward(conv_stride(padded_a, downsampling_filter), 1)
    before_b = normed_b * narrow_norm_gains[1] + narrow_norm_biases[1]
    hidden_b = logistic_squash(before_b)
    standardized_current, spread_c = norm_forward(pointwise_mapping(hidden_b, opening_expander), 2)
    sampled = input_feature_maps[:, ::2, ::2]
    standardized_prior, spread_p = norm_forward(pointwise_mapping(sampled, skip_projection), 3)
    accumulated_total = (
        standardized_current * wide_norm_gains[0]
        + wide_norm_biases[0]
        + (standardized_prior * wide_norm_gains[1] + wide_norm_biases[1])
    )
    return {
        "normed_a": normed_a,
        "spread_a": spread_a,
        "before_a": before_a,
        "padded_a": padded_a,
        "normed_b": normed_b,
        "spread_b": spread_b,
        "before_b": before_b,
        "hidden_b": hidden_b,
        "normed_c": standardized_current,
        "spread_c": spread_c,
        "sampled": sampled,
        "normed_p": standardized_prior,
        "spread_p": spread_p,
        "summed": accumulated_total,
        "output": logistic_squash(accumulated_total),
    }


def layer_one_back(
    kept,
    out_grad,
    input_feature_maps,
    opening_reducer,
    downsampling_filter,
    opening_expander,
    skip_projection,
    narrow_norm_gains,
    wide_norm_gains,
):
    total_grad = out_grad * unit_slope(kept["summed"])
    grad_c, amp_c, base_c = norm_backward(
        total_grad, kept["normed_c"], kept["spread_c"], wide_norm_gains[0], 7)
    grad_p, amp_p, base_p = norm_backward(
        total_grad, kept["normed_p"], kept["spread_p"], wide_norm_gains[1], 8)
    grad_widener = outer_sum(kept["hidden_b"], grad_c)
    grad_shortcut = outer_sum(kept["sampled"], grad_p)
    before_b_grad = project_back(grad_c, opening_expander) * unit_slope(kept["before_b"])
    grad_b, scale_b, offset_b = norm_backward(
        before_b_grad, kept["normed_b"], kept["spread_b"], narrow_norm_gains[1], 9)
    strided, pull_stride = jax.vjp(conv_stride, kept["padded_a"], downsampling_filter)
    padded_grad, grad_strider = pull_stride(grad_b)
    lower_rim = from_behind(padded_grad[:, 0:1], "rows", -1)
    hidden_grad = padded_grad[:, 1:] + jnp.concatenate(
        [jnp.zeros_like(padded_grad[:, 1:-1]), lower_rim], 1
    )
    before_a_grad = hidden_grad * unit_slope(kept["before_a"])
    grad_a, scale_a, offset_a = norm_backward(
        before_a_grad, kept["normed_a"], kept["spread_a"], narrow_norm_gains[0], 10)
    grad_narrower = outer_sum(input_feature_maps, grad_a)
    sample_grad = project_back(grad_p, skip_projection)
    frame_count, row_count, column_count, channel_count = sample_grad.shape
    spread_out = jnp.pad(
        sample_grad[:, :, None, :, None, :], ((0, 0), (0, 0), (0, 1), (0, 0), (0, 1), (0, 0))
    )
    spread_out = spread_out.reshape(frame_count, 2 * row_count, 2 * column_count, channel_count)
    input_grad = project_back(grad_a, opening_reducer) + spread_out
    return {
        "input": input_grad,
        "narrower": grad_narrower,
        "strider": grad_strider,
        "widener": grad_widener,
        "shortcut": grad_shortcut,
        "scales": (scale_a, scale_b),
        "offsets": (offset_a, offset_b),
        "amps": (amp_c, amp_p),
        "bases": (base_c, base_p),
    }


def layer_two(
    above_adjacent,
    closing_reducer,
    excite_reducer,
    excite_spatial_filter,
    excite_expander,
    time_taps,
    spatial_filters,
    closing_expander,
    narrow_norm_gains,
    narrow_norm_biases,
    wide_norm_gains,
    wide_norm_biases,
    earlier_boundary_filter,
    later_boundary_filter,
):
    normed_a, spread_a = norm_forward(pointwise_mapping(above_adjacent, closing_reducer), 4)
    before_a = normed_a * narrow_norm_gains[2] + narrow_norm_biases[2]
    hidden = logistic_squash(before_a)
    reduced = pointwise_mapping(hidden, excite_reducer)
    incoming = from_behind(reduced[0:1], "frames", -1)
    following = jnp.concatenate([reduced[1:], incoming], 0) * later_boundary_filter
    follow_pad = row_padded(following)
    motion = (conv_valid(follow_pad, excite_spatial_filter) - reduced) * later_boundary_filter
    area = motion.shape[1] * motion.shape[2] * lax.axis_size("rows")
    pooled = lax.psum(jnp.sum(motion, axis=(1, 2)), "rows") / area
    gating = jax.nn.sigmoid(jnp.dot(pooled, excite_expander, precision=HIGHEST))
    excited = hidden * (1.0 + gating[:, None, None, :])
    width = excited.shape[-1] // 4
    branches = [excited[..., :width]]
    source_pads = []
    mixed_pads = []
    for index in range(3):
        source = excited[..., (index + 1) * width : (index + 2) * width]
        if index > 0:
            source = source + branches[-1]
        source_pad = frame_padded(source)
        mixed = time_mix(
            source_pad,
            time_taps[:, index * width : (index + 1) * width],
            earlier_boundary_filter,
            later_boundary_filter,
        )
        mixed_pad = row_padded(mixed)
        branches.append(conv_valid(mixed_pad, spatial_filters[index]))
        source_pads.append(source_pad)
        mixed_pads.append(mixed_pad)
    normed_b, spread_b = norm_forward(jnp.concatenate(branches, -1), 5)
    before_b = normed_b * narrow_norm_gains[3] + narrow_norm_biases[3]
    logistic_outcomes = logistic_squash(before_b)
    standardized_current, spread_c = norm_forward(
        pointwise_mapping(logistic_outcomes, closing_expander), 6)
    accumulated_total = (
        standardized_current * wide_norm_gains[2] + wide_norm_biases[2] + above_adjacent
    )
    return {
        "normed_a": normed_a,
        "spread_a": spread_a,
        "before_a": before_a,
        "hidden": hidden,
        "reduced": reduced,
        "follow_pad": follow_pad,
        "pooled": pooled,
        "gating": gating,
        "source_pads": source_pads,
        "mixed_pads": mixed_pads,
        "normed_b": normed_b,
        "spread_b": spread_b,
        "before_b": before_b,
        "squashed": logistic_outcomes,
        "normed_c": standardized_current,
        "spread_c": spread_c,
        "summed": accumulated_total,
        "output": logistic_squash(accumulated_total),
    }


def layer_two_back(
    kept,
    out_grad,
    above_adjacent,
    closing_reducer,
    excite_reducer,
    excite_spatial_filter,
    excite_expander,
    time_taps,
    spatial_filters,
    closing_expander,
    narrow_norm_gains,
    wide_norm_gains,
    earlier_boundary_filter,
    later_boundary_filter,
):
    total_grad = out_grad * unit_slope(kept["summed"])
    grad_c, amp_c, base_c = norm_backward(
        total_grad, kept["normed_c"], kept["spread_c"], wide_norm_gains[2], 11)
    grad_restorer = outer_sum(kept["squashed"], grad_c)
    before_b_grad = project_back(grad_c, closing_expander) * unit_slope(kept["before_b"])
    merged_grad, scale_b, offset_b = norm_backward(
        before_b_grad, kept["normed_b"], kept["spread_b"], narrow_norm_gains[3], 12)
    width = merged_grad.shape[-1] // 4
    group_grads = [merged_grad[..., :width], None, None, None]
    kernel_grads = [None, None, None]
    tap_grads = [None, None, None]
    carried = jnp.zeros_like(merged_grad[..., :width])
    for index in (2, 1, 0):
        branch_grad = merged_grad[..., (index + 1) * width : (index + 2) * width] + carried
        kernel_grads[index] = kernel_grad(
            kept["mixed_pads"][index], spatial_filters[index], branch_grad
        )
        mixed_grad = conv_valid(row_padded(branch_grad), flipped(spatial_filters[index]))
        source_pad = kept["source_pads"][index]
        tap_grads[index] = jnp.stack(
            [
                jnp.sum(mixed_grad * earlier_boundary_filter * source_pad[:-2], axis=(0, 1, 2)),
                jnp.sum(mixed_grad * source_pad[1:-1], axis=(0, 1, 2)),
                jnp.sum(mixed_grad * later_boundary_filter * source_pad[2:], axis=(0, 1, 2)),
            ]
        )
        group_taps = time_taps[:, index * width : (index + 1) * width]
        carried = time_mix(
            frame_padded(mixed_grad),
            group_taps[::-1],
            earlier_boundary_filter,
            later_boundary_filter,
        )
        group_grads[index + 1] = carried
    excited_grad = jnp.concatenate(group_grads, -1)
    gating = kept["gating"]
    hidden = kept["hidden"]
    hidden_grad = excited_grad * (1.0 + gating[:, None, None, :])
    gate_part = jnp.sum(excited_grad * hidden, axis=(1, 2)) * gating * (1.0 - gating)
    grad_exciter = jnp.dot(kept["pooled"].T, gate_part, precision=HIGHEST)
    logit_grad = lax.psum(gate_part, "rows")
    reduced = kept["reduced"]
    area = reduced.shape[1] * reduced.shape[2] * lax.axis_size("rows")
    pooled_grad = jnp.dot(logit_grad, excite_expander.T, precision=HIGHEST) / area
    motion_grad = jnp.broadcast_to(
        pooled_grad[:, None, None, :] * later_boundary_filter, reduced.shape
    )
    grad_stencil = kernel_grad(kept["follow_pad"], excite_spatial_filter, motion_grad)
    follow_grad = (
        conv_valid(row_padded(motion_grad), flipped(excite_spatial_filter)) * later_boundary_filter
    )
    outgoing = from_behind(follow_grad[-1:], "frames", 1)
    reduced_grad = jnp.concatenate([outgoing, follow_grad[:-1]], 0) - motion_grad
    grad_condenser = outer_sum(hidden, reduced_grad)
    hidden_grad = hidden_grad + project_back(reduced_grad, excite_reducer)
    before_a_grad = hidden_grad * unit_slope(kept["before_a"])
    grad_a, scale_a, offset_a = norm_backward(
        before_a_grad, kept["normed_a"], kept["spread_a"], narrow_norm_gains[2], 13)
    grad_squeezer = outer_sum(above_adjacent, grad_a)
    upper_grad = total_grad + project_back(grad_a, closing_reducer)
    return {
        "upper": upper_grad,
        "squeezer": grad_squeezer,
        "condenser": grad_condenser,
        "stencil": grad_stencil,
        "exciter": grad_exciter,
        "temporal": jnp.concatenate(tap_grads, 1),
        "kernels": jnp.stack(kernel_grads),
        "restorer": grad_restorer,
        "scales": (scale_a, scale_b),
        "offsets": (offset_a, offset_b),
        "amp": amp_c,
        "base": base_c,
    }


def flat(matrix):
    return matrix.reshape(-1, matrix.shape[-1])


def unflat(piece, model):
    return piece.reshape(model.shape[:-1] + (piece.shape[-1],))


def shards(
    input_feature_maps,
    sequence_slot_lookup,
    sequence_span_lookup,
    opening_reducer,
    downsampling_filter,
    opening_expander,
    skip_projection,
    closing_reducer,
    excite_reducer,
    excite_spatial_filter,
    excite_expander,
    time_taps,
    spatial_filters,
    closing_expander,
    narrow_norm_gains,
    narrow_norm_biases,
    wide_norm_gains,
    wide_norm_biases,
    loss_slope_wrt_final,
):
    opening_reducer = opening_reducer.astype(jnp.float32)
    downsampling_filter = downsampling_filter.astype(jnp.float32)
    opening_expander = opening_expander.astype(jnp.float32)
    skip_projection = skip_projection.astype(jnp.float32)
    closing_reducer = closing_reducer.astype(jnp.float32)
    excite_reducer = excite_reducer.astype(jnp.float32)
    excite_spatial_filter = excite_spatial_filter.astype(jnp.float32)
    excite_expander = excite_expander.astype(jnp.float32)
    time_taps = time_taps.astype(jnp.float32)
    spatial_filters = spatial_filters.astype(jnp.float32)
    closing_expander = closing_expander.astype(jnp.float32)
    earlier_boundary_filter = (sequence_slot_lookup > 0).astype(jnp.float32)[:, None, None, None]
    later_boundary_filter = (sequence_slot_lookup < sequence_span_lookup - 1).astype(jnp.float32)[
        :, None, None, None
    ]
    first = layer_one(
        input_feature_maps,
        opening_reducer,
        downsampling_filter,
        opening_expander,
        skip_projection,
        narrow_norm_gains,
        narrow_norm_biases,
        wide_norm_gains,
        wide_norm_biases,
    )
    above_adjacent = first["output"]
    again, incoming_grad = above_adjacent, loss_slope_wrt_final
    second = layer_two(
        again,
        closing_reducer,
        excite_reducer,
        excite_spatial_filter,
        excite_expander,
        time_taps,
        spatial_filters,
        closing_expander,
        narrow_norm_gains,
        narrow_norm_biases,
        wide_norm_gains,
        wide_norm_biases,
        earlier_boundary_filter,
        later_boundary_filter,
    )
    second_backward = layer_two_back(
        second,
        incoming_grad,
        again,
        closing_reducer,
        excite_reducer,
        excite_spatial_filter,
        excite_expander,
        time_taps,
        spatial_filters,
        closing_expander,
        narrow_norm_gains,
        wide_norm_gains,
        earlier_boundary_filter,
        later_boundary_filter,
    )
    first_backward = layer_one_back(
        first,
        second_backward["upper"],
        input_feature_maps,
        opening_reducer,
        downsampling_filter,
        opening_expander,
        skip_projection,
        narrow_norm_gains,
        wide_norm_gains,
    )
    pieces = (
        lax.psum_scatter(flat(first_backward["narrower"]), "rows", scatter_dimension=1, tiled=True),
        lax.psum_scatter(flat(first_backward["strider"]), "rows", scatter_dimension=1, tiled=True),
        lax.psum_scatter(flat(first_backward["widener"]), "rows", scatter_dimension=1, tiled=True),
        lax.psum_scatter(flat(first_backward["shortcut"]), "rows", scatter_dimension=1, tiled=True),
        lax.psum_scatter(
            flat(second_backward["squeezer"]), "rows", scatter_dimension=1, tiled=True
        ),
        lax.psum_scatter(
            flat(second_backward["condenser"]), "rows", scatter_dimension=1, tiled=True
        ),
        lax.psum_scatter(flat(second_backward["stencil"]), "rows", scatter_dimension=1, tiled=True),
        lax.psum_scatter(flat(second_backward["exciter"]), "rows", scatter_dimension=1, tiled=True),
        lax.psum_scatter(
            flat(second_backward["temporal"]), "rows", scatter_dimension=1, tiled=True
        ),
        lax.psum_scatter(flat(second_backward["kernels"]), "rows", scatter_dimension=1, tiled=True),
        lax.psum_scatter(
            flat(second_backward["restorer"]), "rows", scatter_dimension=1, tiled=True
        ),
    )
    totals = lax.psum(
        (
            pieces[0],
            pieces[1],
            pieces[2],
            pieces[3],
            pieces[4],
            pieces[5],
            pieces[6],
            pieces[7],
            pieces[8],
            pieces[9],
            pieces[10],
        ),
        "frames",
    )
    grad_scaling = jnp.stack(
        [
            first_backward["scales"][0],
            first_backward["scales"][1],
            second_backward["scales"][0],
            second_backward["scales"][1],
        ]
    )
    grad_biasing = jnp.stack(
        [
            first_backward["offsets"][0],
            first_backward["offsets"][1],
            second_backward["offsets"][0],
            second_backward["offsets"][1],
        ]
    )
    grad_amplitudes = jnp.stack(
        [first_backward["amps"][0], first_backward["amps"][1], second_backward["amp"]]
    )
    baseline_gradient = jnp.stack(
        [first_backward["bases"][0], first_backward["bases"][1], second_backward["base"]]
    )
    return (
        second["output"],
        first_backward["input"],
        unflat(totals[0], opening_reducer),
        unflat(totals[1], downsampling_filter),
        unflat(totals[2], opening_expander),
        unflat(totals[3], skip_projection),
        unflat(totals[4], closing_reducer),
        unflat(totals[5], excite_reducer),
        unflat(totals[6], excite_spatial_filter),
        unflat(totals[7], excite_expander),
        unflat(totals[8], time_taps),
        unflat(totals[9], spatial_filters),
        unflat(totals[10], closing_expander),
        grad_scaling,
        grad_biasing,
        grad_amplitudes,
        baseline_gradient,
    )


def solution(mesh):
    return jax.shard_map(
        shards,
        mesh=mesh,
        in_specs=(
            P("frames", "rows", None, None),
            P("frames"),
            P("frames"),
            P(),
            P(),
            P(),
            P(),
            P(),
            P(),
            P(),
            P(),
            P(),
            P(),
            P(),
            P(),
            P(),
            P(),
            P(),
            P("frames", "rows", None, None),
        ),
        out_specs=(
            P("frames", "rows", None, None),
            P("frames", "rows", None, None),
            P(None, "rows"),
            P(None, None, None, "rows"),
            P(None, "rows"),
            P(None, "rows"),
            P(None, "rows"),
            P(None, "rows"),
            P(None, None, None, "rows"),
            P(None, "rows"),
            P(None, "rows"),
            P(None, None, None, None, "rows"),
            P(None, "rows"),
            P(),
            P(),
            P(),
            P(),
        ),
        check_vma=False,
    )
```

profile of v0, /device:TPU:0, one launch (start us, length us, event | category | flops | bytes accessed | tf_op | source)
XLA Modules:
  0.0 1272.0 jit_solution(3152798160297263306)
XLA Ops:
  15.9 12.8 %shard_map.314 = f32[8,128]{1,0:T(8,128)} custom-call(f32[8,128]{1,0:T(8,128)} %pad_maximum_fusion.38.refs_0_), custom_call_target="tpu_custom_call" | custom-call | tf_op jit(solution)/shard_map/pallas_call | solution.py:144
  37.9 11.2 slice.415
  55.5 10.4 shard_map.317
  110.3 10.5 shard_map.318
  197.7 16.8 %shard_map.319 = f32[8,128]{1,0:T(8,128)} custom-call(f32[8,128]{1,0:T(8,128)} %pad_maximum_fusion.41.refs_0_), custom_call_target="tpu_custom_call" | custom-call | tf_op jit(solution)/shard_map/pallas_call | solution.py:144
  223.2 10.7 shard_map.320
  241.5 10.3 shard_map.321
  259.2 10.3 shard_map.322
  325.7 17.0 %psum.92 = f32[12,512]{1,0:T(8,128)} all-reduce(f32[12,512]{1,0:T(8,128)} %subtract_multiply_fusion.19), channel_id=1, replica_groups=mesh['frames'=8,'rows'=4] {'rows'}, use_global_device_ids=true, to_apply=%region_21.0 | all-reduce | flops 6144 | bytes 49152 | tf_op jit(solution)/shard_map/psum | solution.py:427
  363.2 15.2 %shard_map.323 = f32[8,128]{1,0:T(8,128)} custom-call(f32[8,128]{1,0:T(8,128)} %pad_maximum_fusion.43.refs_0_), custom_call_target="tpu_custom_call" | custom-call | tf_op jit(solution)/shard_map/pallas_call | solution.py:144
  387.6 11.9 shard_map.324
  405.4 11.2 shard_map.325
  425.6 11.3 collective-permute-done.31
  478.2 11.6 shard_map.327
  499.4 13.0 %fusion.4 = f32[3,3,512,512]{3,2,1,0:T(8,128)} fusion(f32[12,5,16,512]{3,2,1,0:T(8,128)} %copy-done.3, f32[12,2,8,512]{3,0,2,1:T(8,128)S(1)} %get-tuple-element.241, f32[512]{0:T(512)S(1)} %get-tuple-element.207, f32[512]{0:T(512)S(1)} %get-tuple-element.206, f32[512]{0:T(512)S(1)} %copy-done.146, f32[512]{0:T(512)S(1)} %copy-done.109, ...), kind=kOutput, calls=%fused_computation.8 | convolution fusion | flops 2606235648 | bytes 12204032 | tf_op jit(solution)/shard_map/transpose(jvp())/conv_general_dilated | solution.py:61
  519.2 60.1 %reduce-scatter.29.cloned.1.call-done = f32[512,512]{1,0:T(8,128)} async-done(((f32[512,2048]{1,0:T(8,128)}), f32[512,512]{1,0:T(8,128)}) %reduce-scatter.29.cloned.1.call-update) | async-done | bytes 1048592 | tf_op jit(solution)/shard_map/reduce_scatter | solution.py:580
  579.2 79.6 %reduce-scatter.17.cloned.1.call-done = f32[512,512]{1,0:T(8,128)} async-done(((f32[512,2048]{1,0:T(8,128)}), f32[512,512]{1,0:T(8,128)}) %reduce-scatter.17.cloned.1.call-update) | async-done | bytes 1048592 | tf_op jit(solution)/shard_map/reduce_scatter | solution.py:566
  658.8 79.4 %reduce-scatter.21.cloned.1.call-done = f32[2048,128]{1,0:T(8,128)} async-done(((f32[2048,512]{1,0:T(8,128)}), f32[2048,128]{1,0:T(8,128)}) %reduce-scatter.21.cloned.1.call-update) | async-done | bytes 1048592 | tf_op jit(solution)/shard_map/reduce_scatter | solution.py:568
  738.2 147.4 %reduce-scatter.19.cloned.1.call-done = f32[1024,512]{0,1:T(8,128)} async-done(((f32[1024,2048]{0,1:T(8,128)}), f32[1024,512]{0,1:T(8,128)}) %reduce-scatter.19.cloned.1.call-update) | async-done | bytes 2097168 | tf_op jit(solution)/shard_map/reduce_scatter | solution.py:567
  885.6 164.5 %reduce-scatter.15.cloned.1.call-done = f32[4608,128]{1,0:T(8,128)} async-done(((f32[4608,512]{1,0:T(8,128)}), f32[4608,128]{1,0:T(8,128)}) %reduce-scatter.15.cloned.1.call-update) | async-done | bytes 2359312 | tf_op jit(solution)/shard_map/reduce_scatter | solution.py:565
  1053.2 19.6 %all-reduce.2 = f32[288,32]{0,1:T(8,128)S(1)} all-reduce(f32[288,32]{0,1:T(8,128)S(1)} %copy.109), channel_id=8, replica_groups=mesh['frames'=8,'rows'=4] {'rows'}, use_global_device_ids=true, to_apply=%region_43.44.clone | all-reduce | flops 9216 | bytes 73728
  1093.7 19.9 %reduce-scatter.23.cloned.1.call-done = f32[512,8]{0,1:T(8,128)} async-done(((f32[512,32]{0,1:T(8,128)}), f32[512,8]{0,1:T(8,128)}) %reduce-scatter.23.cloned.1.call-update) | async-done | bytes 16400 | tf_op jit(solution)/shard_map/reduce_scatter | solution.py:571
  1113.6 25.7 %all-reduce.3 = (f32[512,8]{0,1:T(8,128)}, f32[3,3,32,8]{2,1,0,3:T(4,128)S(1)}, f32[32,128]{1,0:T(8,128)}, f32[3,96]{1,0:T(4,128)}) all-reduce(f32[512,8]{0,1:T(8,128)} %reduce-scatter.23.cloned.1.call-done, f32[3,3,32,8]{2,1,0,3:T(4,128)S(1)} %reshape.861, ...), channel_id=1, replica_groups=mesh['frames'=8,'rows'=4] {'frames'}, use_global_device_ids=true, to_apply=%region_42.43 | all-reduce | flops 10784 | bytes 86272 | tf_op jit(solution)/shard_map/psum | solution.py:584
  1147.4 103.5 %all-reduce.7.cloned.1.call-done = (f32[1024,128]{0,1:T(8,128)}, f32[3,3,512,128]{3,2,1,0:T(8,128)}, f32[512,512]{1,0:T(8,128)}, f32[1024,512]{0,1:T(8,128)}, f3...) async-done(((f32[1024,128]{0,1:T(8,128)}, f32[3,3,512,128]{3,2,1,0:T(8,128)}, f32[512,512]{1,0:T(8,128)}, f32[1024,512]{0,1:T(8,128)}, ...) | async-done | bytes 8568848 | tf_op jit(solution)/shard_map/psum | solution.py:584
  (603 shorter events, 370.9 us)
Async XLA Ops:
  7.2 509.9 %reduce-scatter.27.cloned.1.call-start = ((), (), s32[]{:S(2)}) async-start(), calls=%async_computation.17 | async-start | bytes 2211840 | tf_op jit(solution)/shard_map/reduce_scatter | solution.py:579
  33.9 32.7 %collective-permute-start = (f32[12,1,16,512]{3,2,1,0:T(8,128)S(1)}, f32[12,1,16,512]{3,2,1,0:T(8,128)}, u32[]{:S(2)}, u32[]{:S(2)}) collective-permute-start(f32[12,1,16,512]{3,2,1,0:T(8,128)S(1)} %slice.511), channel_id=1, source_target_pairs={{0,1},{1,2},{2,3},{4,5},{5,6},{6,7},{8,9},{9,10},{10,11},{12,13},{... | collective-permute-start | bytes 1179656 | tf_op jit(solution)/shard_map/ppermute | solution.py:30
  130.0 6.2 collective-permute-start.3
  158.5 6.2 collective-permute-start.7
  172.6 6.2 collective-permute-start.11
  189.8 6.2 collective-permute-start.15
  274.9 6.3 collective-permute-start.17
  291.5 6.2 collective-permute-start.21
  305.4 7.0 collective-permute-start.24
  309.0 6.2 collective-permute-start.25
  317.3 6.4 collective-permute-start.26
  343.7 8.1 collective-permute-start.29
  345.2 6.7 collective-permute-start.28
  359.0 160.1 %reduce-scatter.13.cloned.1.call-start = ((), (), s32[]{:S(2)}) async-start(), calls=%async_computation.10 | async-start | bytes 2621440 | tf_op jit(solution)/shard_map/reduce_scatter | solution.py:564
  423.7 13.2 %collective-permute-start.31 = (f32[12,1,16,512]{3,2,1,0:T(8,128)S(1)}, f32[12,1,16,512]{3,2,1,0:T(8,128)S(1)}, u32[]{:S(2)}, u32[]{:S(2)}) collective-permute-start(f32[12,1,16,512]{3,2,1,0:T(8,128)S(1)} %copy.133), channel_id=1, source_target_pairs={{1,0},{2,1},{3,2},{5,4},{6,5},{7,6},{9,8},{10,9},{11,10},{13,12},{... | collective-permute-start | bytes 1179656 | tf_op jit(solution)/shard_map/ppermute | solution.py:30
  457.4 121.8 %reduce-scatter.29.cloned.1.call-start = ((), (), s32[]{:S(2)}) async-start(), calls=%async_computation.18 | async-start | bytes 5242880 | tf_op jit(solution)/shard_map/reduce_scatter | solution.py:580
  464.5 194.3 %reduce-scatter.17.cloned.1.call-start = ((), (), s32[]{:S(2)}) async-start(), calls=%async_computation.12 | async-start | bytes 5242880 | tf_op jit(solution)/shard_map/reduce_scatter | solution.py:566
  471.6 266.6 %reduce-scatter.21.cloned.1.call-start = ((), (), s32[]{:S(2)}) async-start(), calls=%async_computation.14 | async-start | bytes 5242880 | tf_op jit(solution)/shard_map/reduce_scatter | solution.py:568
  478.1 407.5 %reduce-scatter.19.cloned.1.call-start = ((), (), s32[]{:S(2)}) async-start(), calls=%async_computation.13 | async-start | bytes 10485760 | tf_op jit(solution)/shard_map/reduce_scatter | solution.py:567
  498.4 551.7 %reduce-scatter.15.cloned.1.call-start = ((), (), s32[]{:S(2)}) async-start(), calls=%async_computation.11 | async-start | bytes 11796480 | tf_op jit(solution)/shard_map/reduce_scatter | solution.py:565
  512.6 561.1 %reduce-scatter.31.cloned.1.call-start = ((), (), s32[]{:S(2)}) async-start(), calls=%async_computation.19 | async-start | bytes 245760
  514.0 579.7 %reduce-scatter.25.cloned.1.call-start = ((), (), s32[]{:S(2)}) async-start(), calls=%async_computation.16 | async-start | bytes 81920 | tf_op jit(solution)/shard_map/reduce_scatter | solution.py:575
  515.0 598.7 %reduce-scatter.23.cloned.1.call-start = ((), (), s32[]{:S(2)}) async-start(), calls=%async_computation.15 | async-start | bytes 81920 | tf_op jit(solution)/shard_map/reduce_scatter | solution.py:571
  517.1 733.9 %all-reduce.7.cloned.1.call-start = ((), (), s32[]{:S(2)}) async-start(), calls=%async_computation.20 | async-start | bytes 17432576 | tf_op jit(solution)/shard_map/psum | solution.py:584
  (199 other events, 2678.7 us)
Sparse Core Ops, SparseCore 0:
  359.1 43.5 reduce-scatter.26
  457.6 43.2 reduce-scatter.12
  503.2 76.0 reduce-scatter.28
  581.5 77.2 reduce-scatter.16
  660.9 77.2 reduce-scatter.20
  740.5 144.9 reduce-scatter.18
  888.0 161.9 reduce-scatter.14
  1053.0 20.6 reduce-scatter.30
  1076.5 17.1 reduce-scatter.24
  1096.5 17.1 reduce-scatter.22
  1119.1 131.7 all-reduce.6
where the time goes:
time: 1280 us; the launch traced here: 1270 us
  waiting for transfers between devices  709 us (55%)
  Pallas kernels  162 us (13%)
  matrix products  121 us (9%)
  blocking collectives  72.4 us (6%)
  starting transfers between devices  70.7 us (6%)
  local copies, waits for them, and re-layouts  59.5 us (5%)
  other arithmetic  59.2 us (5%)
  between operations  17.2 us (1%)
    reduce_scatter x1, waiting for transfers between devices, shards(): lax.psum_scatter(flat(first_backward['strider']), 'rows', scatter_dimensi...  165 us
    pallas_call x14, Pallas kernels, global_sum(): pl.pallas_call(lambda *refs: sum_kernel(frames, rows, *refs), out_shape=j...  162 us
    reduce_scatter x1, waiting for transfers between devices, shards(): lax.psum_scatter(flat(first_backward['shortcut']), 'rows', scatter_dimens...  147 us
    psum x1, waiting for transfers between devices, shards(): lax.psum((pieces[0], pieces[1], pieces[2], pieces[3], pieces[4], pieces[5...  104 us
    reduce_scatter x1, waiting for transfers between devices, shards(): lax.psum_scatter(flat(first_backward['widener']), 'rows', scatter_dimensi...  79.6 us
    reduce_scatter x1, waiting for transfers between devices, shards(): lax.psum_scatter(flat(second_backward['squeezer']), 'rows', scatter_dimen...  79.4 us
    reduce_scatter x1, waiting for transfers between devices, shards(): lax.psum_scatter(flat(second_backward['restorer']), 'rows', scatter_dimen...  60.1 us
    ppermute x14, starting transfers between devices, with_halo(): lax.ppermute(lax.slice_in_dim(block, block.shape[dim] - width, None, axis...  41.9 us
  transfers between devices with their start and end apart: 43, of which 29 were waited for; matrix products, arithmetic and copies ran while one was open for 11% of the time, Pallas kernels for 6%

commit v1 on v0

--- a/solution.py
+++ b/solution.py
@@ -1,3 +1,6 @@
+import math
+from types import SimpleNamespace
+
 import jax
 import jax.numpy as jnp
 from jax import lax
@@ -165,6 +168,238 @@
     return results
 
 
+def add_rows(target, source, rows, target_columns=None):
+    step = 8
+    while rows % (2 * step) == 0 and 2 * step * source.shape[-1] <= 32768:
+        step *= 2
+
+    @pl.loop(0, rows // step)
+    def _(place):
+        spot = pl.ds(pl.multiple_of(place * step, step), step)
+        if target_columns is None:
+            target[spot, :] = target[spot, :] + source[spot, :]
+        else:
+            target[spot, target_columns] = target[spot, target_columns] + source[spot, :]
+
+
+def gradient_item(grad, out, bufs, send, recv, place):
+    own, from_core, first_p, first_q, second_p, second_q, third, fourth, final = bufs
+    a_count, b_count, rows, columns = own.shape
+    half, quarter = columns // 2, columns // 4
+    ia, ib, c, r = place
+    f = (ia * b_count + ib) * 2 + c
+    low, high = pl.ds(0, half), pl.ds(half, half)
+    flip1 = r + 1 - 2 * lax.rem(r, 2)
+    flip2 = lax.rem(r + 2, 4)
+    pending = []
+    used = [0]
+
+    def remote(source, target, device):
+        copy = pltpu.make_async_remote_copy(
+            src_ref=source,
+            dst_ref=target,
+            send_sem=send.at[used[0]],
+            recv_sem=recv.at[used[0]],
+            device_id=device,
+            device_id_type=MESH,
+        )
+        used[0] += 1
+        copy.start()
+        pending.append(copy)
+        return copy
+
+    def a_peer(step):
+        other = lax.rem(ia + step, a_count)
+        return other, ((other * b_count + ib) * 2 + c, r)
+
+    def b_peer(step):
+        other = lax.rem(ib + step, b_count)
+        return other, ((ia * b_count + other) * 2 + c, r)
+
+    core = (f + 1 - 2 * c, r)
+    local = pltpu.make_async_copy(grad.at[:, :, c], own, recv.at[used[0]])
+    used[0] += 1
+    local.start()
+    waits = [remote(grad.at[:, :, 1 - c], from_core, core)]
+    yield
+    local.wait()
+    waits[0].wait_recv()
+    for i in range(a_count):
+        for j in range(b_count):
+            add_rows(own.at[i, j], from_core.at[i, j], rows)
+    waits = []
+    for step in range(1, b_count):
+        other, device = b_peer(step)
+        waits.append(remote(own.at[:, other, :, low], first_p.at[step - 1], device))
+    for step in range(1, a_count):
+        other, device = a_peer(step)
+        waits.append(remote(own.at[other, :, :, high], first_q.at[step - 1], device))
+    yield
+    for copy in waits:
+        copy.wait_recv()
+    for step in range(1, b_count):
+        for i in range(a_count):
+            add_rows(own.at[i, ib, :, low], first_p.at[step - 1, i], rows)
+    for step in range(1, a_count):
+        for j in range(b_count):
+            add_rows(own.at[ia, j, :, high], first_q.at[step - 1, j], rows)
+    waits = []
+    for step in range(1, a_count):
+        other, device = a_peer(step)
+        waits.append(remote(own.at[other, ib, :, low], second_p.at[step - 1], device))
+    for step in range(1, b_count):
+        other, device = b_peer(step)
+        waits.append(remote(own.at[ia, other, :, high], second_q.at[step - 1], device))
+    yield
+    for copy in waits:
+        copy.wait_recv()
+    mine = own.at[ia, ib]
+    for step in range(1, a_count):
+        add_rows(mine.at[:, low], second_p.at[step - 1], rows)
+    for step in range(1, b_count):
+        add_rows(mine.at[:, high], second_q.at[step - 1], rows)
+
+    def part(index):
+        return pl.ds(pl.multiple_of(index * quarter, quarter), quarter)
+
+    waits = []
+    for k in range(2):
+        waits.append(remote(mine.at[:, part(lax.rem(flip1, 2) + 2 * k)], third.at[k], (f, flip1)))
+    yield
+    for copy in waits:
+        copy.wait_recv()
+    for k in range(2):
+        add_rows(mine, third.at[k], rows, part(lax.rem(r, 2) + 2 * k))
+    waits = [remote(mine.at[:, part(flip2)], fourth, (f, flip2))]
+    yield
+    waits[0].wait_recv()
+    add_rows(mine, fourth, rows, part(r))
+    piece = mine.at[:, part(r)]
+    cut = rows // 2 if rows % 16 == 0 else rows
+    first, second = pl.ds(0, cut), pl.ds(cut, rows - cut)
+    local = pltpu.make_async_copy(piece, out.at[ia, ib, c], recv.at[used[0]])
+    used[0] += 1
+    local.start()
+    waits = []
+    for step in range(1, b_count):
+        other, device = b_peer(step)
+        waits.append(remote(piece.at[first], out.at[ia, ib, c, first], device))
+    if cut < rows:
+        for step in range(1, a_count):
+            other, device = a_peer(step)
+            waits.append(remote(piece.at[second], out.at[ia, ib, c, second], device))
+    yield
+    local.wait()
+    for copy in waits:
+        copy.wait_recv()
+    waits = []
+    for step in range(1, a_count):
+        other, device = a_peer(step)
+        waits.append(remote(out.at[ia, :, c, first], out.at[ia, :, c, first], device))
+    if cut < rows:
+        for step in range(1, b_count):
+            other, device = b_peer(step)
+            waits.append(remote(out.at[:, ib, c, second], out.at[:, ib, c, second], device))
+    yield
+    for copy in waits:
+        copy.wait_recv()
+    waits = [remote(out.at[:, :, c], out.at[:, :, c], core)]
+    yield
+    waits[0].wait_recv()
+    for copy in pending:
+        copy.wait_send()
+
+
+def gradient_kernel(splits, counts, *refs):
+    a_count, b_count = counts
+    grads, refs = refs[: len(splits)], refs[len(splits) :]
+    outs, refs = refs[: len(splits)], refs[len(splits) :]
+    f = lax.axis_index("frames")
+    r = lax.axis_index("rows")
+    c = lax.rem(f, 2)
+    ib = lax.rem(f // 2, b_count)
+    ia = f // (2 * b_count)
+    partners = [
+        (f + 1 - 2 * c, r),
+        (f, r + 1 - 2 * lax.rem(r, 2)),
+        (f, lax.rem(r + 2, 4)),
+    ]
+    for step in range(1, b_count):
+        partners.append(((ia * b_count + lax.rem(ib + step, b_count)) * 2 + c, r))
+    for step in range(1, a_count):
+        partners.append(((lax.rem(ia + step, a_count) * b_count + ib) * 2 + c, r))
+    barrier = pltpu.get_barrier_semaphore()
+    for partner in partners:
+        pl.semaphore_signal(barrier, inc=1, device_id=partner, device_id_type=MESH)
+    pl.semaphore_wait(barrier, len(partners))
+    waiting = []
+    for index, split in enumerate(splits):
+        for k in range(split):
+            bufs, refs = refs[:9], refs[9:]
+            send, recv, refs = refs[0], refs[1], refs[2:]
+            waiting.append(
+                gradient_item(
+                    grads[index].at[k], outs[index].at[k], bufs, send, recv, (ia, ib, c, r)
+                )
+            )
+    active = []
+    while waiting or active:
+        running = []
+        for item in active:
+            if next(item, active) is None:
+                running.append(item)
+        if waiting:
+            item = waiting.pop(0)
+            next(item)
+            running.append(item)
+        active = running
+
+
+def sum_gradients(grads, call):
+    frames = lax.axis_size("frames")
+    levels = int(math.log2(frames // 2))
+    b_count = 2 ** (levels // 2)
+    a_count = frames // 2 // b_count
+    operands, results, scratch = [], [], []
+    copies = 8 + 2 * (a_count - 1) * 2 + 2 * (b_count - 1) * 2
+    for grad, split in grads:
+        depth, columns = grad.shape
+        rows = depth // (split * frames)
+        operands.append(grad.reshape(split, a_count, b_count, 2, rows, columns))
+        results.append(
+            jax.ShapeDtypeStruct((split, a_count, b_count, 2, rows, columns // 4), jnp.float32)
+        )
+        for _ in range(split):
+            for shape in (
+                (a_count, b_count, rows, columns),
+                (a_count, b_count, rows, columns),
+                (b_count - 1, a_count, rows, columns // 2),
+                (a_count - 1, b_count, rows, columns // 2),
+                (a_count - 1, rows, columns // 2),
+                (b_count - 1, rows, columns // 2),
+                (2, rows, columns // 4),
+                (rows, columns // 4),
+                (8, 128),
+            ):
+                scratch.append(pltpu.VMEM(shape, jnp.float32))
+            scratch += [pltpu.SemaphoreType.DMA((copies,)), pltpu.SemaphoreType.DMA((copies,))]
+    splits = [split for _, split in grads]
+    totals = pl.pallas_call(
+        lambda *refs: gradient_kernel(splits, (a_count, b_count), *refs),
+        out_shape=results,
+        in_specs=[pl.BlockSpec(memory_space=pl.ANY)] * len(grads),
+        out_specs=[pl.BlockSpec(memory_space=pl.ANY)] * len(grads),
+        scratch_shapes=scratch,
+        compiler_params=pltpu.CompilerParams(
+            collective_id=call, has_side_effects=True, vmem_limit_bytes=60 * 2**20
+        ),
+    )(*operands)
+    return [
+        total.reshape(grad.shape[0], grad.shape[1] // 4)
+        for total, (grad, _) in zip(totals, grads)
+    ]
+
+
 def global_count(field):
     return (
         field.shape[0]
@@ -221,23 +456,23 @@
         + wide_norm_biases[0]
         + (standardized_prior * wide_norm_gains[1] + wide_norm_biases[1])
     )
-    return {
-        "normed_a": normed_a,
-        "spread_a": spread_a,
-        "before_a": before_a,
-        "padded_a": padded_a,
-        "normed_b": normed_b,
-        "spread_b": spread_b,
-        "before_b": before_b,
-        "hidden_b": hidden_b,
-        "normed_c": standardized_current,
-        "spread_c": spread_c,
-        "sampled": sampled,
-        "normed_p": standardized_prior,
-        "spread_p": spread_p,
-        "summed": accumulated_total,
-        "output": logistic_squash(accumulated_total),
-    }
+    return SimpleNamespace(
+        normed_a=normed_a,
+        spread_a=spread_a,
+        before_a=before_a,
+        padded_a=padded_a,
+        normed_b=normed_b,
+        spread_b=spread_b,
+        before_b=before_b,
+        hidden_b=hidden_b,
+        normed_c=standardized_current,
+        spread_c=spread_c,
+        sampled=sampled,
+        normed_p=standardized_prior,
+        spread_p=spread_p,
+        summed=accumulated_total,
+        output=logistic_squash(accumulated_total),
+    )
 
 
 def layer_one_back(
@@ -251,25 +486,25 @@
     narrow_norm_gains,
     wide_norm_gains,
 ):
-    total_grad = out_grad * unit_slope(kept["summed"])
+    total_grad = out_grad * unit_slope(kept.summed)
     grad_c, amp_c, base_c = norm_backward(
-        total_grad, kept["normed_c"], kept["spread_c"], wide_norm_gains[0], 7)
+        total_grad, kept.normed_c, kept.spread_c, wide_norm_gains[0], 7)
     grad_p, amp_p, base_p = norm_backward(
-        total_grad, kept["normed_p"], kept["spread_p"], wide_norm_gains[1], 8)
-    grad_widener = outer_sum(kept["hidden_b"], grad_c)
-    grad_shortcut = outer_sum(kept["sampled"], grad_p)
-    before_b_grad = project_back(grad_c, opening_expander) * unit_slope(kept["before_b"])
+        total_grad, kept.normed_p, kept.spread_p, wide_norm_gains[1], 8)
+    grad_widener = outer_sum(kept.hidden_b, grad_c)
+    grad_shortcut = outer_sum(kept.sampled, grad_p)
+    before_b_grad = project_back(grad_c, opening_expander) * unit_slope(kept.before_b)
     grad_b, scale_b, offset_b = norm_backward(
-        before_b_grad, kept["normed_b"], kept["spread_b"], narrow_norm_gains[1], 9)
-    strided, pull_stride = jax.vjp(conv_stride, kept["padded_a"], downsampling_filter)
+        before_b_grad, kept.normed_b, kept.spread_b, narrow_norm_gains[1], 9)
+    strided, pull_stride = jax.vjp(conv_stride, kept.padded_a, downsampling_filter)
     padded_grad, grad_strider = pull_stride(grad_b)
     lower_rim = from_behind(padded_grad[:, 0:1], "rows", -1)
     hidden_grad = padded_grad[:, 1:] + jnp.concatenate(
         [jnp.zeros_like(padded_grad[:, 1:-1]), lower_rim], 1
     )
-    before_a_grad = hidden_grad * unit_slope(kept["before_a"])
+    before_a_grad = hidden_grad * unit_slope(kept.before_a)
     grad_a, scale_a, offset_a = norm_backward(
-        before_a_grad, kept["normed_a"], kept["spread_a"], narrow_norm_gains[0], 10)
+        before_a_grad, kept.normed_a, kept.spread_a, narrow_norm_gains[0], 10)
     grad_narrower = outer_sum(input_feature_maps, grad_a)
     sample_grad = project_back(grad_p, skip_projection)
     frame_count, row_count, column_count, channel_count = sample_grad.shape
@@ -278,17 +513,17 @@
     )
     spread_out = spread_out.reshape(frame_count, 2 * row_count, 2 * column_count, channel_count)
     input_grad = project_back(grad_a, opening_reducer) + spread_out
-    return {
-        "input": input_grad,
-        "narrower": grad_narrower,
-        "strider": grad_strider,
-        "widener": grad_widener,
-        "shortcut": grad_shortcut,
-        "scales": (scale_a, scale_b),
-        "offsets": (offset_a, offset_b),
-        "amps": (amp_c, amp_p),
-        "bases": (base_c, base_p),
-    }
+    return SimpleNamespace(
+        input=input_grad,
+        narrower=grad_narrower,
+        strider=grad_strider,
+        widener=grad_widener,
+        shortcut=grad_shortcut,
+        scales=(scale_a, scale_b),
+        offsets=(offset_a, offset_b),
+        amps=(amp_c, amp_p),
+        bases=(base_c, base_p),
+    )
 
 
 def layer_two(
@@ -346,26 +581,26 @@
     accumulated_total = (
         standardized_current * wide_norm_gains[2] + wide_norm_biases[2] + above_adjacent
     )
-    return {
-        "normed_a": normed_a,
-        "spread_a": spread_a,
-        "before_a": before_a,
-        "hidden": hidden,
-        "reduced": reduced,
-        "follow_pad": follow_pad,
-        "pooled": pooled,
-        "gating": gating,
-        "source_pads": source_pads,
-        "mixed_pads": mixed_pads,
-        "normed_b": normed_b,
-        "spread_b": spread_b,
-        "before_b": before_b,
-        "squashed": logistic_outcomes,
-        "normed_c": standardized_current,
-        "spread_c": spread_c,
-        "summed": accumulated_total,
-        "output": logistic_squash(accumulated_total),
-    }
+    return SimpleNamespace(
+        normed_a=normed_a,
+        spread_a=spread_a,
+        before_a=before_a,
+        hidden=hidden,
+        reduced=reduced,
+        follow_pad=follow_pad,
+        pooled=pooled,
+        gating=gating,
+        source_pads=source_pads,
+        mixed_pads=mixed_pads,
+        normed_b=normed_b,
+        spread_b=spread_b,
+        before_b=before_b,
+        squashed=logistic_outcomes,
+        normed_c=standardized_current,
+        spread_c=spread_c,
+        summed=accumulated_total,
+        output=logistic_squash(accumulated_total),
+    )
 
 
 def layer_two_back(
@@ -384,13 +619,13 @@
     earlier_boundary_filter,
     later_boundary_filter,
 ):
-    total_grad = out_grad * unit_slope(kept["summed"])
+    total_grad = out_grad * unit_slope(kept.summed)
     grad_c, amp_c, base_c = norm_backward(
-        total_grad, kept["normed_c"], kept["spread_c"], wide_norm_gains[2], 11)
-    grad_restorer = outer_sum(kept["squashed"], grad_c)
-    before_b_grad = project_back(grad_c, closing_expander) * unit_slope(kept["before_b"])
+        total_grad, kept.normed_c, kept.spread_c, wide_norm_gains[2], 11)
+    grad_restorer = outer_sum(kept.squashed, grad_c)
+    before_b_grad = project_back(grad_c, closing_expander) * unit_slope(kept.before_b)
     merged_grad, scale_b, offset_b = norm_backward(
-        before_b_grad, kept["normed_b"], kept["spread_b"], narrow_norm_gains[3], 12)
+        before_b_grad, kept.normed_b, kept.spread_b, narrow_norm_gains[3], 12)
     width = merged_grad.shape[-1] // 4
     group_grads = [merged_grad[..., :width], None, None, None]
     kernel_grads = [None, None, None]
@@ -399,10 +634,10 @@
     for index in (2, 1, 0):
         branch_grad = merged_grad[..., (index + 1) * width : (index + 2) * width] + carried
         kernel_grads[index] = kernel_grad(
-            kept["mixed_pads"][index], spatial_filters[index], branch_grad
+            kept.mixed_pads[index], spatial_filters[index], branch_grad
         )
         mixed_grad = conv_valid(row_padded(branch_grad), flipped(spatial_filters[index]))
-        source_pad = kept["source_pads"][index]
+        source_pad = kept.source_pads[index]
         tap_grads[index] = jnp.stack(
             [
                 jnp.sum(mixed_grad * earlier_boundary_filter * source_pad[:-2], axis=(0, 1, 2)),
@@ -419,19 +654,19 @@
         )
         group_grads[index + 1] = carried
     excited_grad = jnp.concatenate(group_grads, -1)
-    gating = kept["gating"]
-    hidden = kept["hidden"]
+    gating = kept.gating
+    hidden = kept.hidden
     hidden_grad = excited_grad * (1.0 + gating[:, None, None, :])
     gate_part = jnp.sum(excited_grad * hidden, axis=(1, 2)) * gating * (1.0 - gating)
-    grad_exciter = jnp.dot(kept["pooled"].T, gate_part, precision=HIGHEST)
+    grad_exciter = jnp.dot(kept.pooled.T, gate_part, precision=HIGHEST)
     logit_grad = lax.psum(gate_part, "rows")
-    reduced = kept["reduced"]
+    reduced = kept.reduced
     area = reduced.shape[1] * reduced.shape[2] * lax.axis_size("rows")
     pooled_grad = jnp.dot(logit_grad, excite_expander.T, precision=HIGHEST) / area
     motion_grad = jnp.broadcast_to(
         pooled_grad[:, None, None, :] * later_boundary_filter, reduced.shape
     )
-    grad_stencil = kernel_grad(kept["follow_pad"], excite_spatial_filter, motion_grad)
+    grad_stencil = kernel_grad(kept.follow_pad, excite_spatial_filter, motion_grad)
     follow_grad = (
         conv_valid(row_padded(motion_grad), flipped(excite_spatial_filter)) * later_boundary_filter
     )
@@ -439,29 +674,34 @@
     reduced_grad = jnp.concatenate([outgoing, follow_grad[:-1]], 0) - motion_grad
     grad_condenser = outer_sum(hidden, reduced_grad)
     hidden_grad = hidden_grad + project_back(reduced_grad, excite_reducer)
-    before_a_grad = hidden_grad * unit_slope(kept["before_a"])
+    before_a_grad = hidden_grad * unit_slope(kept.before_a)
     grad_a, scale_a, offset_a = norm_backward(
-        before_a_grad, kept["normed_a"], kept["spread_a"], narrow_norm_gains[2], 13)
+        before_a_grad, kept.normed_a, kept.spread_a, narrow_norm_gains[2], 13)
     grad_squeezer = outer_sum(above_adjacent, grad_a)
     upper_grad = total_grad + project_back(grad_a, closing_reducer)
-    return {
-        "upper": upper_grad,
-        "squeezer": grad_squeezer,
-        "condenser": grad_condenser,
-        "stencil": grad_stencil,
-        "exciter": grad_exciter,
-        "temporal": jnp.concatenate(tap_grads, 1),
-        "kernels": jnp.stack(kernel_grads),
-        "restorer": grad_restorer,
-        "scales": (scale_a, scale_b),
-        "offsets": (offset_a, offset_b),
-        "amp": amp_c,
-        "base": base_c,
-    }
+    return SimpleNamespace(
+        upper=upper_grad,
+        squeezer=grad_squeezer,
+        condenser=grad_condenser,
+        stencil=grad_stencil,
+        exciter=grad_exciter,
+        temporal=jnp.concatenate(tap_grads, 1),
+        kernels=jnp.stack(kernel_grads),
+        restorer=grad_restorer,
+        scales=(scale_a, scale_b),
+        offsets=(offset_a, offset_b),
+        amp=amp_c,
+        base=base_c,
+    )
 
 
 def flat(matrix):
     return matrix.reshape(-1, matrix.shape[-1])
+
+
+def by_column(matrix):
+    pieces = matrix.reshape(matrix.shape[0], 4, -1).transpose(1, 0, 2)
+    return pieces.reshape(4, -1, 128).transpose(1, 0, 2).reshape(-1, 512)
 
 
 def unflat(piece, model):
@@ -515,7 +755,7 @@
         wide_norm_gains,
         wide_norm_biases,
     )
-    above_adjacent = first["output"]
+    above_adjacent = first.output
     again, incoming_grad = above_adjacent, loss_slope_wrt_final
     second = layer_two(
         again,
@@ -551,7 +791,7 @@
     )
     first_backward = layer_one_back(
         first,
-        second_backward["upper"],
+        second_backward.upper,
         input_feature_maps,
         opening_reducer,
         downsampling_filter,
@@ -560,79 +800,73 @@
         narrow_norm_gains,
         wide_norm_gains,
     )
-    pieces = (
-        lax.psum_scatter(flat(first_backward["narrower"]), "rows", scatter_dimension=1, tiled=True),
-        lax.psum_scatter(flat(first_backward["strider"]), "rows", scatter_dimension=1, tiled=True),
-        lax.psum_scatter(flat(first_backward["widener"]), "rows", scatter_dimension=1, tiled=True),
-        lax.psum_scatter(flat(first_backward["shortcut"]), "rows", scatter_dimension=1, tiled=True),
-        lax.psum_scatter(
-            flat(second_backward["squeezer"]), "rows", scatter_dimension=1, tiled=True
+    kernels = second_backward.kernels.reshape(4, -1, 4, second_backward.kernels.shape[-1] // 4)
+    packed = jnp.concatenate(
+        [
+            kernels.transpose(1, 2, 0, 3).reshape(kernels.shape[1], -1),
+            by_column(second_backward.condenser),
+            by_column(flat(second_backward.stencil)),
+            by_column(second_backward.exciter),
+            by_column(jnp.pad(second_backward.temporal.reshape(3, 4, -1), ((0, 0), (0, 0), (0, 32))).reshape(3, -1)),
+        ],
+        0,
+    )
+    packed = jnp.pad(packed, ((0, -packed.shape[0] % 128 if packed.shape[0] > 1024 else 1024 - packed.shape[0]), (0, 0)))
+    totals = sum_gradients(
+        (
+            (first_backward.shortcut, 2),
+            (flat(first_backward.strider), 3),
+            (first_backward.widener, 1),
+            (second_backward.restorer, 1),
+            (second_backward.squeezer, 1),
+            (first_backward.narrower, 1),
+            (packed, 1),
         ),
-        lax.psum_scatter(
-            flat(second_backward["condenser"]), "rows", scatter_dimension=1, tiled=True
-        ),
-        lax.psum_scatter(flat(second_backward["stencil"]), "rows", scatter_dimension=1, tiled=True),
-        lax.psum_scatter(flat(second_backward["exciter"]), "rows", scatter_dimension=1, tiled=True),
-        lax.psum_scatter(
-            flat(second_backward["temporal"]), "rows", scatter_dimension=1, tiled=True
-        ),
-        lax.psum_scatter(flat(second_backward["kernels"]), "rows", scatter_dimension=1, tiled=True),
-        lax.psum_scatter(
-            flat(second_backward["restorer"]), "rows", scatter_dimension=1, tiled=True
-        ),
-    )
-    totals = lax.psum(
-        (
-            pieces[0],
-            pieces[1],
-            pieces[2],
-            pieces[3],
-            pieces[4],
-            pieces[5],
-            pieces[6],
-            pieces[7],
-            pieces[8],
-            pieces[9],
-            pieces[10],
-        ),
-        "frames",
-    )
+        14,
+    )
+    tail = totals[6]
+    start = kernels.shape[1]
+    grad_kernels = tail[:start].reshape(start, 4, -1).transpose(1, 0, 2).reshape(spatial_filters.shape[:-1] + (-1,))
+    grad_condenser = tail[start : start + 32].reshape(excite_reducer.shape[0], -1)
+    grad_stencil = tail[start + 32 : start + 50].reshape(excite_spatial_filter.shape[:-1] + (-1,))
+    grad_exciter = tail[start + 50 : start + 82]
+    grad_temporal = tail[start + 82 : start + 85, :96]
     grad_scaling = jnp.stack(
         [
-            first_backward["scales"][0],
-            first_backward["scales"][1],
-            second_backward["scales"][0],
-            second_backward["scales"][1],
+            first_backward.scales[0],
+            first_backward.scales[1],
+            second_backward.scales[0],
+            second_backward.scales[1],
         ]
     )
     grad_biasing = jnp.stack(
         [
-            first_backward["offsets"][0],
-            first_backward["offsets"][1],
-            second_backward["offsets"][0],
-            second_backward["offsets"][1],
+            first_backward.offsets[0],
+            first_backward.offsets[1],
+            second_backward.offsets[0],
+            second_backward.offsets[1],
         ]
     )
     grad_amplitudes = jnp.stack(
-        [first_backward["amps"][0], first_backward["amps"][1], second_backward["amp"]]
+        [first_backward.amps[0], first_backward.amps[1], second_backward.amp]
     )
     baseline_gradient = jnp.stack(
-        [first_backward["bases"][0], first_backward["bases"][1], second_backward["base"]]
+        [first_backward.bases[0], first_backward.bases[1], second_backward.base]
     )
     return (
-        second["output"],
-        first_backward["input"],
-        unflat(totals[0], opening_reducer),
+        second.output,
+        first_backward.input,
+        totals[5],
         unflat(totals[1], downsampling_filter),
-        unflat(totals[2], opening_expander),
-        unflat(totals[3], skip_projection),
-        unflat(totals[4], closing_reducer),
-        unflat(totals[5], excite_reducer),
-        unflat(totals[6], excite_spatial_filter),
-        unflat(totals[7], excite_expander),
-        unflat(totals[8], time_taps),
-        unflat(totals[9], spatial_filters),
-        unflat(totals[10], closing_expander),
+        totals[2],
+        totals[0],
+        totals[4],
+        grad_condenser,
+        grad_stencil,
+        grad_exciter,
+        grad_temporal,
+        grad_kernels,
+        totals[3],
         grad_scaling,
         grad_biasing,
         grad_amplitudes,

time: 1280 us -> 772 us (0.60)
  waiting for transfers between devices: 709 us -> 17 us
  Pallas kernels: 162 us -> 357 us
  blocking collectives: 72.4 us -> 30.2 us
  local copies, waits for them, and re-layouts: 59.5 us -> 92.8 us
  matrix products: 121 us -> 107 us
  between operations: 17.2 us -> 3.67 us
  starting transfers between devices: 70.7 us -> 83.9 us
    reduce_scatter x9 -> x0, waiting for transfers between devices: 553 us -> none  [the longest x1 165 us: shards(): lax.psum_scatter(flat(first_backward['strider']), 'rows', scatter_dimensi...]
    pallas_call x0 -> x1, Pallas kernels: none -> 197 us  [sum_gradients(): pl.pallas_call(lambda *refs: gradient_kernel(splits, (a_count, b_count),...]
    psum x1 -> x0, waiting for transfers between devices: 104 us -> none  [shards(): lax.psum((pieces[0], pieces[1], pieces[2], pieces[3], pieces[4], pieces[5...]
    ppermute x14, waiting for transfers between devices: 34.2 us -> 7.98 us  [with_halo(): lax.ppermute(lax.slice_in_dim(block, 0, width, axis=dim), axis, backward)]
    psum x1 -> x0, blocking collectives: 25.7 us -> none  [shards(): lax.psum((pieces[0], pieces[1], pieces[2], pieces[3], pieces[4], pieces[5...]
    unnamed x1 -> x0, blocking collectives: 19.6 us -> none
    ppermute x14, starting transfers between devices: 41.9 us -> 56.9 us  [with_halo(): lax.ppermute(lax.slice_in_dim(block, block.shape[dim] - width, None, axis...]
    unnamed x374 -> x375, local copies, waits for them, and re-layouts: 29.2 us -> 24.9 us
  transfers between devices with their start and end apart: 43 -> 32, of which waited for: 29 -> 12; matrix products, arithmetic and copies ran while one was open for 11% -> 10% of each run, Pallas kernels for 6% -> 1%
where the time goes in v1:
time: 772 us; the launch traced here: 760 us
  Pallas kernels  357 us (46%)
  matrix products  107 us (14%)
  local copies, waits for them, and re-layouts  92.8 us (12%)
  starting transfers between devices  83.9 us (11%)
  other arithmetic  68.6 us (9%)
  blocking collectives  30.2 us (4%)
  waiting for transfers between devices  17 us (2%)
    pallas_call x1, Pallas kernels, sum_gradients(): pl.pallas_call(lambda *refs: gradient_kernel(splits, (a_count, b_count),...  197 us
    pallas_call x14, Pallas kernels, global_sum(): pl.pallas_call(lambda *refs: sum_kernel(frames, rows, *refs), out_shape=j...  159 us
    ppermute x14, starting transfers between devices, with_halo(): lax.ppermute(lax.slice_in_dim(block, block.shape[dim] - width, None, axis...  56.9 us
    dot_general x6, matrix products, outer_sum(): return jnp.einsum('fhwc,fhwd->cd', active, grads, precision=HIGHEST)  26.4 us
    unnamed x375, local copies, waits for them, and re-layouts  24.9 us
    dot_general x6, matrix products, project_back(): return jnp.einsum('fhwd,cd->fhwc', grads, matrix, precision=HIGHEST)  23.4 us
    dot_general x6, matrix products, pointwise_mapping(): return jnp.einsum('fhwc,cd->fhwd', active, matrix, precision=HIGHEST)  21.9 us
    conv_general_dilated x3, matrix products, conv_stride(): lax.conv_general_dilated(padded, kernel, (2, 2), ((0, 0), (1, 1)), dimens...  20.5 us
  transfers between devices with their start and end apart: 32, of which 12 were waited for; matrix products, arithmetic and copies ran while one was open for 10% of the time, Pallas kernels for 1%

profile of v1, /device:TPU:0, one launch (start us, length us, event | category | flops | bytes accessed | tf_op | source)
XLA Modules:
  0.0 760.1 jit_solution(11688968860772959949)
XLA Ops:
  9.4 12.8 %shard_map.314 = f32[8,128]{1,0:T(8,128)} custom-call(f32[8,128]{1,0:T(8,128)} %pad_maximum_fusion.37.refs_0_), custom_call_target="tpu_custom_call" | custom-call | tf_op jit(solution)/shard_map/pallas_call | solution.py:147
  31.3 11.2 %slice.430 = f32[12,2,8,1024]{3,2,1,0:T(8,128)S(1)} slice(f32[12,4,16,1024]{3,2,1,0:T(8,128)} %param.19), slice={[0:12:1], [0:4:2], [0:16:2], [0:1024:1]} | slice | bytes 1572864 | tf_op jit(solution)/shard_map/slice | solution.py:452
  49.0 10.4 %shard_map.317 = f32[32,128]{1,0:T(8,128)} custom-call(f32[32,128]{1,0:T(8,128)} %pad_maximum_fusion.32.refs_0_), custom_call_target="tpu_custom_call" | custom-call | tf_op jit(solution)/shard_map/pallas_call | solution.py:147
  61.8 6.5 fusion.159
  68.8 10.2 %shard_map.315 = f32[8,128]{1,0:T(8,128)} custom-call(f32[8,128]{1,0:T(8,128)} %pad_maximum_fusion.38.refs_0_), custom_call_target="tpu_custom_call" | custom-call | tf_op jit(solution)/shard_map/pallas_call | solution.py:147
  86.5 10.1 %shard_map.316 = f32[32,128]{1,0:T(8,128)} custom-call(f32[32,128]{1,0:T(8,128)} %pad_maximum_fusion.31.refs_0_), custom_call_target="tpu_custom_call" | custom-call | tf_op jit(solution)/shard_map/pallas_call | solution.py:147
  103.8 10.5 %shard_map.318 = f32[8,128]{1,0:T(8,128)} custom-call(f32[8,128]{1,0:T(8,128)} %pad_maximum_fusion.39.refs_0_), custom_call_target="tpu_custom_call" | custom-call | tf_op jit(solution)/shard_map/pallas_call | solution.py:147
  129.8 11.9 %psum.14 = f32[12,32]{1,0:T(8,128)S(1)} all-reduce(f32[12,32]{1,0:T(8,128)S(1)} %fusion.102), channel_id=1, replica_groups=mesh['frames'=8,'rows'=4] {'rows'}, use_global_device_ids=true, to_apply=%region_11.0 | all-reduce | flops 384 | bytes 3072 | tf_op jit(solution)/shard_map/psum | solution.py:554
  193.8 16.3 %shard_map.319 = f32[8,128]{1,0:T(8,128)} custom-call(f32[8,128]{1,0:T(8,128)} %pad_maximum_fusion.40.refs_0_), custom_call_target="tpu_custom_call" | custom-call | tf_op jit(solution)/shard_map/pallas_call | solution.py:147
  218.7 10.7 %shard_map.320 = f32[32,128]{1,0:T(8,128)} custom-call(f32[32,128]{1,0:T(8,128)} %pad_maximum_fusion.33.refs_0_), custom_call_target="tpu_custom_call" | custom-call | tf_op jit(solution)/shard_map/pallas_call | solution.py:147
  237.1 10.6 %shard_map.321 = f32[32,128]{1,0:T(8,128)} custom-call(f32[32,128]{1,0:T(8,128)} %pad_maximum_fusion.34.refs_0_), custom_call_target="tpu_custom_call" | custom-call | tf_op jit(solution)/shard_map/pallas_call | solution.py:147
  255.1 10.4 %shard_map.322 = f32[8,128]{1,0:T(8,128)} custom-call(f32[8,128]{1,0:T(8,128)} %pad_maximum_fusion.41.refs_0_), custom_call_target="tpu_custom_call" | custom-call | tf_op jit(solution)/shard_map/pallas_call | solution.py:147
  338.9 18.3 %psum.15 = f32[12,512]{1,0:T(8,128)} all-reduce(f32[12,512]{1,0:T(8,128)S(1)} %subtract_multiply_fusion.19), channel_id=1, replica_groups=mesh['frames'=8,'rows'=4] {'rows'}, use_global_device_ids=true, to_apply=%region_21.0 | all-reduce | flops 6144 | bytes 49152 | tf_op jit(solution)/shard_map/psum | solution.py:662
  387.1 13.6 %shard_map.323 = f32[8,128]{1,0:T(8,128)} custom-call(f32[8,128]{1,0:T(8,128)} %pad_maximum_fusion.42.refs_0_), custom_call_target="tpu_custom_call" | custom-call | tf_op jit(solution)/shard_map/pallas_call | solution.py:147
  403.5 6.3 multiply_reduce_fusion.2
  410.4 10.8 %shard_map.324 = f32[32,128]{1,0:T(8,128)} custom-call(f32[32,128]{1,0:T(8,128)} %get-tuple-element.153.refs_0_), custom_call_target="tpu_custom_call" | custom-call | tf_op jit(solution)/shard_map/pallas_call | solution.py:147
  427.7 10.3 %shard_map.325 = f32[8,128]{1,0:T(8,128)} custom-call(f32[8,128]{1,0:T(8,128)} %pad_maximum_fusion.43.refs_0_), custom_call_target="tpu_custom_call" | custom-call | tf_op jit(solution)/shard_map/pallas_call | solution.py:147
  439.4 6.1 fusion.103
  448.6 7.9 %fusion.4 = f32[3,3,512,512]{3,2,1,0:T(8,128)} fusion(f32[12,5,16,512]{3,2,1,0:T(8,128)S(1)} %copy-done.4, f32[12,2,8,512]{3,0,2,1:T(8,128)S(1)} %get-tuple-element.212, f32[512]{0:T(512)S(1)} %get-tuple-element.178, f32[512]{0:T(512)S(1)} %get-tuple-element.177, f32[512]{0:T(512)S(1)} %copy-done.161, f32[512]{0:T(512)S(1)} %copy-done.117, ...), kind=kOutput, calls=%fused_computation.4 | convolution fusion | flops 2606235648 | bytes 12204032 | tf_op jit(solution)/shard_map/transpose(jvp())/conv_general_dilated | solution.py:64
  466.1 10.5 %shard_map.327 = f32[32,128]{1,0:T(8,128)} custom-call(f32[32,128]{1,0:T(8,128)} %get-tuple-element.154.refs_0_), custom_call_target="tpu_custom_call" | custom-call | tf_op jit(solution)/shard_map/pallas_call | solution.py:147
  504.5 5.9 fusion.86
  514.5 12.1 %shard_map.326 = f32[8,128]{1,0:T(8,128)} custom-call(f32[8,128]{1,0:T(8,128)} %pad_maximum_fusion.44.refs_0_), custom_call_target="tpu_custom_call" | custom-call | tf_op jit(solution)/shard_map/pallas_call | solution.py:147
  527.4 6.5 convolution_bitcast_fusion
  536.7 197.2 %shard_map.328 = (f32[2,2,2,2,64,512]{5,4,3,2,1,0:T(8,128)}, f32[3,2,2,2,192,128]{5,4,3,2,1,0:T(8,128)}, f32[1,2,2,2,64,512]{5,4,3,2,1,0:T(8,128)}, f32[1,2,2,2,...) custom-call(f32[2,2,2,2,64,2048]{5,4,3,2,1,0:T(8,128)} %bitcast.376,, ...), custom_call_target="tpu_custom_call" | custom-call | tf_op jit(solution)/shard_map/pallas_call | solution.py:387
  (596 shorter events, 319.3 us)
Async XLA Ops:
  27.3 32.8 %collective-permute-start = (f32[12,1,16,512]{3,2,1,0:T(8,128)S(1)}, f32[12,1,16,512]{3,2,1,0:T(8,128)}, u32[]{:S(2)}, u32[]{:S(2)}) collective-permute-start(f32[12,1,16,512]{3,2,1,0:T(8,128)S(1)} %slice.531), channel_id=1, source_target_pairs={{0,1},{1,2},{2,3},{4,5},{5,6},{6,7},{8,9},{9,10},{10,11},{12,13},{... | collective-permute-start | bytes 1179656 | tf_op jit(solution)/shard_map/ppermute | solution.py:33
  121.0 6.6 collective-permute-start.3
  122.3 6.3 collective-permute-start.2
  152.1 6.3 collective-permute-start.7
  153.5 6.4 collective-permute-start.6
  167.7 6.5 collective-permute-start.11
  169.0 6.8 collective-permute-start.10
  184.0 6.7 collective-permute-start.15
  185.3 6.8 collective-permute-start.14
  268.3 6.5 collective-permute-start.17
  269.6 6.4 collective-permute-start.16
  276.6 9.5 %collective-permute-start.19 = (f32[1,2,8,128]{3,0,2,1:T(1,128)S(1)}, f32[1,2,8,128]{3,0,2,1:T(1,128)S(1)}, u32[]{:S(2)}, u32[]{:S(2)}) collective-permute-start(f32[1,2,8,128]{3,0,2,1:T(1,128)S(1)} %get-tuple-element.116), channel_id=1, source_target_pairs={{4,0},{8,4},{12,8},{16,12},{20,16},{24,20},{28,24},{5,1},{9,5},{13... | collective-permute-start | bytes 24584 | tf_op jit(solution)/shard_map/ppermute | solution.py:25
  278.0 8.1 %collective-permute-start.18 = (f32[1,2,8,128]{3,0,2,1:T(1,128)S(1)}, f32[1,2,8,128]{3,0,2,1:T(1,128)S(1)}, u32[]{:S(2)}, u32[]{:S(2)}) collective-permute-start(f32[1,2,8,128]{3,0,2,1:T(1,128)S(1)} %get-tuple-element.115), channel_id=1, source_target_pairs={{0,4},{4,8},{8,12},{12,16},{16,20},{20,24},{24,28},{1,5},{5,9},{9,... | collective-permute-start | bytes 24584 | tf_op jit(solution)/shard_map/ppermute | solution.py:22
  287.5 7.5 collective-permute-start.21
  288.8 7.4 collective-permute-start.20
  296.7 5.7 collective-permute-start.23
  303.9 21.0 %collective-permute-start.25 = (f32[12,1,8,128]{3,0,2,1:T(8,128)}, f32[12,1,8,128]{3,0,2,1:T(8,128)}, u32[]{:S(2)}, u32[]{:S(2)}) collective-permute-start(f32[12,1,8,128]{3,0,2,1:T(8,128)} %get-tuple-element.110), channel_id=1, source_target_pairs={{1,0},{2,1},{3,2},{5,4},{6,5},{7,6},{9,8},{10,9},{11,10},{13,12},{... | collective-permute-start | bytes 147464 | tf_op jit(solution)/shard_map/ppermute | solution.py:25
  305.2 19.7 %collective-permute-start.24 = (f32[12,1,8,128]{3,0,2,1:T(8,128)}, f32[12,1,8,128]{3,0,2,1:T(8,128)}, u32[]{:S(2)}, u32[]{:S(2)}) collective-permute-start(f32[12,1,8,128]{3,0,2,1:T(8,128)} %get-tuple-element.109), channel_id=1, source_target_pairs={{0,1},{1,2},{2,3},{4,5},{5,6},{6,7},{8,9},{9,10},{10,11},{12,13},{... | collective-permute-start | bytes 147464 | tf_op jit(solution)/shard_map/ppermute | solution.py:22
  327.3 7.5 collective-permute-start.27
  328.6 6.2 collective-permute-start.26
  358.1 8.6 %collective-permute-start.29 = (f32[12,1,8,32]{3,2,1,0:T(8,128)S(1)}, f32[12,1,8,32]{3,2,1,0:T(8,128)S(1)}, u32[]{:S(2)}, u32[]{:S(2)}) collective-permute-start(f32[12,1,8,32]{3,2,1,0:T(8,128)S(1)} %slice.511), channel_id=1, source_target_pairs={{1,0},{2,1},{3,2},{5,4},{6,5},{7,6},{9,8},{10,9},{11,10},{13,12},{... | collective-permute-start | bytes 36872 | tf_op jit(solution)/shard_map/ppermute | solution.py:25
  359.4 7.3 collective-permute-start.28
  369.2 13.8 %collective-permute-start.30 = (f32[1,2,8,32]{3,2,1,0:T(8,128)}, f32[1,2,8,32]{3,2,1,0:T(8,128)}, u32[]{:S(2)}, u32[]{:S(2)}) collective-permute-start(f32[1,2,8,32]{3,2,1,0:T(8,128)} %slice.577), channel_id=1, source_target_pairs={{0,4},{4,8},{8,12},{12,16},{16,20},{20,24},{24,28},{1,5},{5,9},{9,... | collective-permute-start | bytes 6152 | tf_op jit(solution)/shard_map/ppermute | solution.py:33
  493.1 17.3 %collective-permute-start.31 = (f32[12,1,16,512]{3,2,1,0:T(8,128)}, f32[12,1,16,512]{3,2,1,0:T(8,128)}, u32[]{:S(2)}, u32[]{:S(2)}) collective-permute-start(f32[12,1,16,512]{3,2,1,0:T(8,128)} %copy.125), channel_id=1, source_target_pairs={{1,0},{2,1},{3,2},{5,4},{6,5},{7,6},{9,8},{10,9},{11,10},{13,12},{... | collective-permute-start | bytes 1179656 | tf_op jit(solution)/shard_map/ppermute | solution.py:33
  (188 other events, 2541.0 us)
